TPU v7x, 32 devices: a whole 2x2x4 slice. The times are simulated.
32 devices in a mesh: rows: 8 (over z, y), seq: 4 (over x, core).
Axes of the slice: x: 2, y: 2, z: 4, core: 2. Of those that a mesh axis runs over, the one named last changes fastest.
Arguments:
- inputs: bfloat16 [32, 1024, 768], P('rows', 'seq'), may hold values from -6 to 6
- segment_ids: int32 [32, 1024], P('rows'), may hold values from 0 to 3, as said below
- gain_one: float32 [768], replicated, may hold values from 0.1 to 1.9
- w_query: bfloat16 [768, 768], replicated, may hold values from -0.4375 to 0.4375
- w_key: bfloat16 [768, 768], replicated, may hold values from -0.21875 to 0.21875
- w_value: bfloat16 [768, 768], replicated, may hold values from -0.21875 to 0.21875
- w_out: bfloat16 [768, 768], replicated, may hold values from -0.875 to 0.875
- mix_logits: bfloat16 [12, 12], replicated, may hold values from -1.75 to 1.75
- mix_weights: bfloat16 [12, 12], replicated, may hold values from -1.75 to 1.75
- gain_two: float32 [768], replicated, may hold values from 0.1 to 1.9
- w_hidden: bfloat16 [768, 3072], replicated, may hold values from -0.21875 to 0.21875
- w_back: bfloat16 [3072, 768], replicated, may hold values from -0.15625 to 0.15625
- cotangent: bfloat16 [32, 1024, 768], P('rows', 'seq'), may hold values from -6 to 6
Outputs:
- block_out: bfloat16 [32, 1024, 768], P('rows', 'seq')
- grad_inputs: bfloat16 [32, 1024, 768], P('rows', 'seq')
- grad_gain_one: float32 [768], replicated
- grad_w_query: float32 [768, 768], replicated
- grad_w_key: float32 [768, 768], replicated
- grad_w_value: float32 [768, 768], replicated
- grad_w_out: float32 [768, 768], replicated
- grad_mix_logits: float32 [12, 12], replicated
- grad_mix_weights: float32 [12, 12], replicated
- grad_gain_two: float32 [768], replicated
- grad_w_hidden: float32 [768, 3072], replicated
- grad_w_back: float32 [3072, 768], replicated
Inputs may be any that keep to these rules, and one draw needn't show every extreme that they name: `segment_ids`: in each row the ids never fall and name four documents 0, 1, 2, 3, each nonempty; document 2 starts before token 256, and document 3 starts at token 3 * (256) or later.
All inputs are finite; a program needn't handle non-finite values.
Results may differ from a plain program's by a relative error of at most 0.017.
The roundings to bfloat16 on the way count: a program that leaves them out, or rounds other values in their place, can miss the bound.
Values may be sent and summed in bfloat16 or wider, within the bound.
No kernel may reach another device: no remote copies, remote signals or barrier semaphores. Data moves between devices by JAX's collectives and lax.ppermute only.
A program may use at most 320 MiB of HBM per device.

v0:
```python
from functools import partial

import jax
import jax.numpy as jnp
from jax import lax
from jax.sharding import PartitionSpec as P

D = 768
H = 12
DH = 64
LEN = 1024
QBLOCK = 512


epsilon = 1e-06


def forward_dot(left, right):
    return jnp.dot(left, right, preferred_element_type=jnp.float32)


def cross_rows(left, right):
    return lax.dot_general(
        left, right, (((0,), (0,)), ((), ())), preferred_element_type=jnp.float32
    )


def against(left, right):
    return lax.dot_general(
        left, right, (((1,), (1,)), ((), ())), preferred_element_type=jnp.float32
    )


def norm_parts(values, gain):
    inverse = lax.rsqrt(jnp.mean(values * values, axis=-1, keepdims=True) + epsilon)
    return (values * inverse * gain, inverse)


def norm_back(values, inverse, gain, upstream):
    weighted = upstream * gain
    grad_gain = jnp.sum(upstream * values * inverse, axis=0)
    grad_values = inverse * weighted - values * inverse * inverse * inverse * jnp.mean(
        weighted * values, axis=-1, keepdims=True
    )
    return (grad_values, grad_gain)


def block_scores(query_row, key_heads, id_row, offset, mix_logits):
    score_scale = DH ** (-0.5)
    query_block = lax.dynamic_slice_in_dim(query_row, offset, QBLOCK, 0).reshape(QBLOCK, H, DH)
    block_ids = lax.dynamic_slice_in_dim(id_row, offset, QBLOCK, 0)
    block_pos = offset + jnp.arange(QBLOCK, dtype=jnp.int32)
    positions = jnp.arange(LEN, dtype=jnp.int32)
    scores = (
        jnp.einsum("qhd,khd->hqk", query_block, key_heads, preferred_element_type=jnp.float32)
        * score_scale
    ).astype(jnp.bfloat16)
    logits = jnp.einsum("hqk,hj->jqk", scores, mix_logits, preferred_element_type=jnp.float32)
    allowed = (block_pos[:, None] >= positions[None, :]) & (block_ids[:, None] == id_row[None, :])
    logits = jnp.where(allowed[None], logits, -1e30)
    return (query_block, scores, logits)


def per_device(
    inputs,
    segment_ids,
    gain_one,
    w_query,
    w_key,
    w_value,
    w_out,
    mix_logits,
    mix_weights,
    gain_two,
    w_hidden,
    w_back,
    cotangent,
):
    seq_devices = lax.axis_size("seq")
    own_rows = inputs.shape[0] // seq_devices
    own_ids = lax.dynamic_slice_in_dim(segment_ids, lax.axis_index("seq") * own_rows, own_rows, 0)
    working_in, working_cot = (inputs, cotangent)
    row_count, local_len, features = working_in.shape
    shaped = (row_count, local_len, features)
    score_scale = DH ** (-0.5)
    offsets = jnp.arange(LEN // QBLOCK, dtype=jnp.int32) * QBLOCK
    flat_in = working_in.astype(jnp.float32).reshape(-1, features)
    normed_f, inverse_one = norm_parts(flat_in, gain_one)
    normed = normed_f.astype(jnp.bfloat16)
    queries = forward_dot(normed, w_query).astype(jnp.bfloat16).reshape(shaped)
    keys_in = forward_dot(normed, w_key).astype(jnp.bfloat16).reshape(shaped)
    values_in = forward_dot(normed, w_value).astype(jnp.bfloat16).reshape(shaped)
    queries_rows, keys_rows, values_rows = (
        lax.all_to_all(queries, "seq", split_axis=0, concat_axis=1, tiled=True),
        lax.all_to_all(keys_in, "seq", split_axis=0, concat_axis=1, tiled=True),
        lax.all_to_all(values_in, "seq", split_axis=0, concat_axis=1, tiled=True),
    )

    def forward_row(packed):
        query_row, key_row, value_row, id_row = packed
        key_heads = key_row.reshape(LEN, H, DH)
        value_heads = value_row.reshape(LEN, H, DH)

        def one_block(offset):
            query_block, scores, logits = block_scores(
                query_row, key_heads, id_row, offset, mix_logits
            )
            row_max = jnp.max(logits, axis=-1, keepdims=True)
            shifted = jnp.exp(logits - row_max)
            row_total = jnp.sum(shifted, axis=-1, keepdims=True)
            soft_low = (shifted / row_total).astype(jnp.bfloat16)
            log_totals = (row_max + jnp.log(row_total))[:, :, 0]
            blended = jnp.einsum(
                "jqk,ji->iqk", soft_low, mix_weights, preferred_element_type=jnp.float32
            ).astype(jnp.bfloat16)
            result = jnp.einsum(
                "iqk,kid->qid", blended, value_heads, preferred_element_type=jnp.float32
            )
            return (result.astype(jnp.bfloat16).reshape(QBLOCK, D), log_totals)

        block_outs, log_totals = lax.map(one_block, offsets)
        return (block_outs.reshape(LEN, D), log_totals)

    attended, log_totals = lax.map(forward_row, (queries_rows, keys_rows, values_rows, own_ids))
    attended_local = lax.all_to_all(attended, "seq", split_axis=1, concat_axis=0, tiled=True)
    attended_flat = attended_local.reshape(-1, features)
    middle = flat_in + forward_dot(attended_flat, w_out)
    normed_two_f, inverse_two = norm_parts(middle, gain_two)
    normed_two = normed_two_f.astype(jnp.bfloat16)
    hidden = forward_dot(normed_two, w_hidden)
    activated = jax.nn.gelu(hidden, approximate=True).astype(jnp.bfloat16)
    block_out = (middle + forward_dot(activated, w_back)).astype(jnp.bfloat16).reshape(shaped)
    grad_top = working_cot.reshape(-1, features)
    grad_w_back = cross_rows(activated, grad_top)
    grad_act = against(grad_top, w_back)
    unused, gelu_pull = jax.vjp(partial(jax.nn.gelu, approximate=True), hidden)
    grad_hidden = gelu_pull(grad_act)[0].astype(jnp.bfloat16)
    grad_w_hidden = cross_rows(normed_two, grad_hidden)
    grad_n2 = against(grad_hidden, w_hidden)
    grad_middle_norm, grad_gain_two = norm_back(middle, inverse_two, gain_two, grad_n2)
    grad_middle = grad_top.astype(jnp.float32) + grad_middle_norm
    grad_attn = grad_middle.astype(jnp.bfloat16)
    grad_w_out = cross_rows(attended_flat, grad_attn)
    grad_attended = against(grad_attn, w_out).astype(jnp.bfloat16).reshape(shaped)
    grad_rows = lax.all_to_all(grad_attended, "seq", split_axis=0, concat_axis=1, tiled=True)

    def backward_row(packed):
        query_row, key_row, value_row, id_row, totals_row, grad_row = packed
        key_heads = key_row.reshape(LEN, H, DH)
        value_heads = value_row.reshape(LEN, H, DH)

        def block_step(running, block_in):
            offset, totals_block = block_in
            grad_keys, grad_values, grad_ml, grad_mw = running
            query_block, scores, logits = block_scores(
                query_row, key_heads, id_row, offset, mix_logits
            )
            softmax = jnp.exp(logits - totals_block[:, :, None])
            soft_low = softmax.astype(jnp.bfloat16)
            blended = jnp.einsum(
                "jqk,ji->iqk", soft_low, mix_weights, preferred_element_type=jnp.float32
            ).astype(jnp.bfloat16)
            grad_out = lax.dynamic_slice_in_dim(grad_row, offset, QBLOCK, 0).reshape(QBLOCK, H, DH)
            grad_blended = jnp.einsum(
                "qid,kid->iqk", grad_out, value_heads, preferred_element_type=jnp.float32
            ).astype(jnp.bfloat16)
            grad_soft = jnp.einsum(
                "iqk,ji->jqk", grad_blended, mix_weights, preferred_element_type=jnp.float32
            )
            grad_mw = grad_mw + jnp.einsum(
                "jqk,iqk->ji", soft_low, grad_blended, preferred_element_type=jnp.float32
            )
            grad_logits = (
                softmax * (grad_soft - jnp.sum(softmax * grad_soft, axis=-1, keepdims=True))
            ).astype(jnp.bfloat16)
            grad_ml = grad_ml + jnp.einsum(
                "hqk,jqk->hj", scores, grad_logits, preferred_element_type=jnp.float32
            )
            grad_scores = jnp.einsum(
                "jqk,hj->hqk", grad_logits, mix_logits, preferred_element_type=jnp.float32
            ).astype(jnp.bfloat16)
            grad_query = (
                jnp.einsum(
                    "hqk,khd->qhd", grad_scores, key_heads, preferred_element_type=jnp.float32
                )
                * score_scale
            )
            grad_keys = (
                grad_keys
                + jnp.einsum(
                    "hqk,qhd->khd", grad_scores, query_block, preferred_element_type=jnp.float32
                )
                * score_scale
            )
            grad_values = grad_values + jnp.einsum(
                "iqk,qid->kid", blended, grad_out, preferred_element_type=jnp.float32
            )
            return (
                (grad_keys, grad_values, grad_ml, grad_mw),
                grad_query.astype(jnp.bfloat16).reshape(QBLOCK, D),
            )

        starting = (
            jnp.zeros((LEN, H, DH), jnp.float32),
            jnp.zeros((LEN, H, DH), jnp.float32),
            jnp.zeros((H, H), jnp.float32),
            jnp.zeros((H, H), jnp.float32),
        )
        finished, grad_query_blocks = lax.scan(block_step, starting, (offsets, totals_row))
        grad_keys, grad_values, grad_ml, grad_mw = finished
        return (
            grad_query_blocks.reshape(LEN, D),
            grad_keys.astype(jnp.bfloat16).reshape(LEN, D),
            grad_values.astype(jnp.bfloat16).reshape(LEN, D),
            grad_ml,
            grad_mw,
        )

    grad_q_rows, grad_k_rows, grad_v_rows, grad_ml_rows, grad_mw_rows = lax.map(
        backward_row, (queries_rows, keys_rows, values_rows, own_ids, log_totals, grad_rows)
    )
    grad_mix_logits = jnp.sum(grad_ml_rows, axis=0)
    grad_mix_weights = jnp.sum(grad_mw_rows, axis=0)
    grad_q_local, grad_k_local, grad_v_local = (
        lax.all_to_all(grad_q_rows, "seq", split_axis=1, concat_axis=0, tiled=True),
        lax.all_to_all(grad_k_rows, "seq", split_axis=1, concat_axis=0, tiled=True),
        lax.all_to_all(grad_v_rows, "seq", split_axis=1, concat_axis=0, tiled=True),
    )
    grad_q_flat = grad_q_local.reshape(-1, features)
    grad_k_flat = grad_k_local.reshape(-1, features)
    grad_v_flat = grad_v_local.reshape(-1, features)
    grad_w_query = cross_rows(normed, grad_q_flat)
    grad_w_key = cross_rows(normed, grad_k_flat)
    grad_w_value = cross_rows(normed, grad_v_flat)
    grad_normed = (
        against(grad_q_flat, w_query) + against(grad_k_flat, w_key) + against(grad_v_flat, w_value)
    )
    grad_in_norm, grad_gain_one = norm_back(flat_in, inverse_one, gain_one, grad_normed)
    grad_inputs = (grad_middle + grad_in_norm).astype(jnp.bfloat16).reshape(shaped)
    (
        grad_gain_one,
        grad_w_query,
        grad_w_key,
        grad_w_value,
        grad_w_out,
        grad_mix_logits,
        grad_mix_weights,
        grad_gain_two,
        grad_w_hidden,
        grad_w_back,
    ) = lax.psum(
        (
            grad_gain_one,
            grad_w_query,
            grad_w_key,
            grad_w_value,
            grad_w_out,
            grad_mix_logits,
            grad_mix_weights,
            grad_gain_two,
            grad_w_hidden,
            grad_w_back,
        ),
        ("rows", "seq"),
    )
    return (
        block_out,
        grad_inputs,
        grad_gain_one,
        grad_w_query,
        grad_w_key,
        grad_w_value,
        grad_w_out,
        grad_mix_logits,
        grad_mix_weights,
        grad_gain_two,
        grad_w_hidden,
        grad_w_back,
    )


def solution(mesh):
    in_specs = (
        P("rows", "seq", None),
        P("rows", None),
        P(),
        P(),
        P(),
        P(),
        P(),
        P(),
        P(),
        P(),
        P(),
        P(),
        P("rows", "seq", None),
    )
    out_specs = (
        P("rows", "seq", None),
        P("rows", "seq", None),
        P(),
        P(),
        P(),
        P(),
        P(),
        P(),
        P(),
        P(),
        P(),
        P(),
    )
    return jax.shard_map(
        per_device, mesh=mesh, in_specs=in_specs, out_specs=out_specs, check_vma=False
    )
```

profile of v0, /device:TPU:0, one launch (start us, length us, event | category | flops | bytes accessed | tf_op | source)
XLA Modules:
  0.0 1592.8 jit_solution(3838417099766963286)
XLA Ops:
  22.6 15.8 all-to-all-done.2
  47.0 15.9 all-to-all-done.1
  80.8 6.6 all-to-all-done
  91.2 243.0 %while.55 = (s32[]{:T(128)}, bf16[2,512,768]{2,1,0:T(8,128)(2,1)}, f32[2,12,512]{1,2,0:T(8,128)}, s32[2]{0:T(128)S(1)}, s32[1024]{0:T(1024)S(1)}, /*index=5*/bf1...) while((s32[]{:T(128)}, bf16[2,512,768]{2,1,0:T(8,128)(2,1)}, ...), condition=%wide.region_4.5_spmd, body=%wide.region_1.4_spmd.sunk | while | flops 1990060544 | bytes 138386192 | solution.py:121
  113.2 6.3 multiply_convert_fusion.12
  119.5 39.6 %bitcast_reduce_fusion.2 = (f32[12,512]{0,1:T(8,128)S(1)}, f32[512,1024,12]{1,2,0:T(8,128)}) fusion(pred[512,1024]{1,0:T(8,128)(4,1)S(1)} %fusion.193, bf16[12,12]{0,1:T(8,128)(2,1)S(1)} %get-tuple-element.613, bf16[12,512,1024]{2,1,0:T(8,128)(2,1)} %multiply_convert_fusion.12), kind=kOutput, calls=%fused_computation.1.clone.1 | convolution fusion | flops 163571712 | bytes 38297888 | tf_op jit(solution)/shard_map/while/body/eval_jaxpr/while/body/eval_jaxpr/hqk,hj->jqk/dot_general | solution.py:58
  159.2 16.1 %fusion.194 = f32[12,512]{0,1:T(8,128)} fusion(f32[512,1024,12]{1,2,0:T(8,128)} %get-tuple-element.561, f32[12,512]{0,1:T(8,128)S(1)} %get-tuple-element.562, pred[512,1024]{1,0:T(8,128)(4,1)S(1)} %fusion.193), kind=kLoop, calls=%fused_computation.4.clone.1 | loop fusion | flops 18868224 | bytes 25739264 | tf_op jit(solution)/shard_map/while/body/eval_jaxpr/while/body/eval_jaxpr/reduce_sum | solution.py:110
  175.3 22.8 %convert_bitcast_fusion.6 = bf16[12,512,1024]{2,0,1:T(8,128)(2,1)} fusion(f32[512,1024,12]{1,2,0:T(8,128)} %get-tuple-element.561, f32[12,512]{0,1:T(8,128)} %fusion.194, f32[12,512]{0,1:T(8,128)S(1)} %get-tuple-element.562, pred[512,1024]{1,0:T(8,128)(4,1)S(1)} %fusion.193, bf16[12,12]{0,1:T(8,128)(2,1)S(1)} %get-tuple-element.614), kind=kOutput, calls=%fused_computation.8.clone.1 | convolution fusion | flops 182452224 | bytes 38322464 | tf_op jit(solution)/shard_map/while/body/eval_jaxpr/while/body/eval_jaxpr/jqk,ji->iqk/dot_general | solution.py:113
  198.1 14.7 fusion.195
  222.1 6.3 multiply_convert_fusion.12
  228.4 39.6 %bitcast_reduce_fusion.2 = (f32[12,512]{0,1:T(8,128)S(1)}, f32[512,1024,12]{1,2,0:T(8,128)}) fusion(pred[512,1024]{1,0:T(8,128)(4,1)S(1)} %fusion.193, bf16[12,12]{0,1:T(8,128)(2,1)S(1)} %get-tuple-element.613, bf16[12,512,1024]{2,1,0:T(8,128)(2,1)} %multiply_convert_fusion.12), kind=kOutput, calls=%fused_computation.1.clone.1 | convolution fusion | flops 163571712 | bytes 38297888 | tf_op jit(solution)/shard_map/while/body/eval_jaxpr/while/body/eval_jaxpr/hqk,hj->jqk/dot_general | solution.py:58
  268.0 16.1 %fusion.194 = f32[12,512]{0,1:T(8,128)} fusion(f32[512,1024,12]{1,2,0:T(8,128)} %get-tuple-element.561, f32[12,512]{0,1:T(8,128)S(1)} %get-tuple-element.562, pred[512,1024]{1,0:T(8,128)(4,1)S(1)} %fusion.193), kind=kLoop, calls=%fused_computation.4.clone.1 | loop fusion | flops 18868224 | bytes 25739264 | tf_op jit(solution)/shard_map/while/body/eval_jaxpr/while/body/eval_jaxpr/reduce_sum | solution.py:110
  284.2 22.8 %convert_bitcast_fusion.6 = bf16[12,512,1024]{2,0,1:T(8,128)(2,1)} fusion(f32[512,1024,12]{1,2,0:T(8,128)} %get-tuple-element.561, f32[12,512]{0,1:T(8,128)} %fusion.194, f32[12,512]{0,1:T(8,128)S(1)} %get-tuple-element.562, pred[512,1024]{1,0:T(8,128)(4,1)S(1)} %fusion.193, bf16[12,12]{0,1:T(8,128)(2,1)S(1)} %get-tuple-element.614), kind=kOutput, calls=%fused_computation.8.clone.1 | convolution fusion | flops 182452224 | bytes 38322464 | tf_op jit(solution)/shard_map/while/body/eval_jaxpr/while/body/eval_jaxpr/jqk,ji->iqk/dot_general | solution.py:113
  306.9 14.7 fusion.195
  334.2 5.5 copy.200
  340.3 12.3 reduce.1
  356.3 24.9 %all_to_all.32 = bf16[4,2,98304]{2,1,0:T(2,128)(2,1)} all-to-all(bf16[4,2,98304]{2,1,0:T(2,128)(2,1)} %reshape.354), channel_id=1, replica_groups=mesh['rows'=8,'seq'=4] {'seq'}, dimensions={0} | all-to-all | bytes 3145728 | tf_op jit(solution)/shard_map/all_to_all | solution.py:125
  390.2 11.7 fusion.112
  401.9 15.4 fusion.71
  417.4 8.3 multiply_reduce_fusion
  437.2 17.0 %all-to-all-done.4 = bf16[4,256,768]{2,1,0:T(8,128)(2,1)} async-done(((bf16[4,256,768]{2,1,0:T(8,128)(2,1)}), bf16[4,256,768]{2,1,0:T(8,128)(2,1)}, u32[]{:S(2)}, u32[]{:S(2)}) %all-to-all-start.4) | async-done | bytes 1572896 | tf_op jit(solution)/shard_map/all_to_all | solution.py:145
  455.5 544.5 %while.56 = (s32[]{:T(128)}, f32[1024,12,64]{0,2,1:T(8,128)}, f32[1024,12,64]{0,2,1:T(8,128)}, f32[12,12]{1,0:T(8,128)}, f32[12,12]{1,0:T(8,128)}, /*index=5*/bf...) while((s32[]{:T(128)}, f32[1024,12,64]{0,2,1:T(8,128)}, ...), condition=%wide.region_9.10_spmd.clone, body=%wide.region_7.9_spmd.clone.sunk | while | flops 5064616960 | bytes 484961344 | solution.py:209
  463.7 8.1 multiply_convert_fusion.13
  471.8 6.4 convolution_convert_fusion.6
  478.3 23.6 %fusion.216 = f32[512,1024,12]{1,2,0:T(8,128)} fusion(bf16[12,512,1024]{2,1,0:T(8,128)(2,1)} %multiply_convert_fusion.13, bf16[12,12]{1,0:T(8,128)(2,1)S(1)} %get-tuple-element.665), kind=kOutput, calls=%fused_computation.38.clone.1 | convolution fusion | flops 150994944 | bytes 37749024 | tf_op jit(solution)/shard_map/while/body/eval_jaxpr/while/body/eval_jaxpr/hqk,hj->jqk/dot_general | solution.py:58
  501.8 20.1 %fusion.221 = bf16[12,512,1024]{2,0,1:T(8,128)(2,1)} fusion(f32[512,1024,12]{1,2,0:T(8,128)} %fusion.216, f32[12,512]{0,1:T(8,128)S(1)} %dynamic-slice_bitcast_fusion.2, pred[512,1024]{1,0:T(8,128)(4,1)S(1)} %fusion.217), kind=kLoop, calls=%fused_computation.31.clone.clone.clone.clone.clone.clone.1.clone.1 | loop fusion | flops 18874368 | bytes 38297600 | tf_op jit(solution)/shard_map/while/body/eval_jaxpr/while/body/eval_jaxpr/jqk,iqk->ji/dot_general | solution.py:170
  521.9 16.9 %fusion.222 = f32[12,12]{1,0:T(8,128)S(1)} fusion(bf16[12,512,1024]{2,1,0:T(8,128)(2,1)} %convolution_convert_fusion.6, f32[12,12]{1,0:T(8,128)S(1)} %copy-done.37, pred[]{:T(512)S(6)} %compare.3, bf16[12,512,1024]{2,0,1:T(8,128)(2,1)} %fusion.221), kind=kOutput, calls=%fused_computation.56.clone.2 | convolution fusion | flops 150995232 | bytes 25166976 | tf_op jit(solution)/shard_map/while/body/eval_jaxpr/while/body/eval_jaxpr/jqk,iqk->ji/dot_general | solution.py:170
  538.8 21.9 %convert_bitcast_fusion.8 = bf16[12,512,1024]{2,0,1:T(8,128)(2,1)} fusion(f32[512,1024,12]{1,2,0:T(8,128)} %fusion.216, f32[12,512]{0,1:T(8,128)S(1)} %dynamic-slice_bitcast_fusion.2, pred[512,1024]{1,0:T(8,128)(4,1)S(1)} %fusion.217, bf16[12,12]{0,1:T(8,128)(2,1)S(1)} %get-tuple-element.669), kind=kOutput, calls=%fused_computation.40.clone.1 | convolution fusion | flops 176160768 | bytes 38297888 | tf_op jit(solution)/shard_map/while/body/eval_jaxpr/while/body/eval_jaxpr/jqk,ji->iqk/dot_general | solution.py:160
  560.7 21.2 %bitcast_add_fusion.6 = f32[1024,12,64]{0,2,1:T(8,128)} fusion(f32[1024,12,64]{0,2,1:T(8,128)} %get-tuple-element.639, bf16[512,12,64]{0,2,1:T(8,128)(2,1)S(1)} %bitcast.308, bf16[12,512,1024]{2,0,1:T(8,128)(2,1)} %convert_bitcast_fusion.8, pred[]{:T(512)S(6)} %compare.3), kind=kOutput, calls=%fused_computation.49.clone.1 | convolution fusion | flops 806879232 | bytes 19660800 | tf_op jit(solution)/shard_map/while/body/eval_jaxpr/while/body/eval_jaxpr/iqk,qid->kid/dot_general | solution.py:195
  581.9 48.7 %fusion.218 = (f32[12,512]{0,1:T(8,128)S(1)}, f32[512,1024,12]{1,2,0:T(8,128)}) fusion(f32[512,1024,12]{1,2,0:T(8,128)} %fusion.216, f32[12,512]{0,1:T(8,128)S(1)} %dynamic-slice_bitcast_fusion.2, pred[512,1024]{1,0:T(8,128)(4,1)S(1)} %fusion.217, bf16[12,12]{0,1:T(8,128)(2,1)S(1)} %get-tuple-element.669, ...), kind=kOutput, calls=%fused_computation.25.clone.1 | convolution fusion | flops 176154624 | bytes 63488288 | tf_op jit(solution)/shard_map/while/body/eval_jaxpr/while/body/eval_jaxpr/iqk,ji->jqk/dot_general | solution.py:167
  630.6 27.7 %fusion.219 = bf16[12,512,1024]{2,0,1:T(8,128)(2,1)} fusion(f32[512,1024,12]{1,2,0:T(8,128)} %get-tuple-element.578, f32[512,1024,12]{1,2,0:T(8,128)} %fusion.216, f32[12,512]{0,1:T(8,128)S(1)} %get-tuple-element.579, f32[12,512]{0,1:T(8,128)S(1)} %dynamic-slice_bitcast_fusion.2, pred[512,1024]{1,0:T(8,128)(4,1)S(1)} %fusion.217), kind=kLoop, calls=%fused_computation.27.clone.1 | loop fusion | flops 31457280 | bytes 63488000 | tf_op jit(solution)/shard_map/while/body/eval_jaxpr/while/body/eval_jaxpr/convert_element_type | solution.py:175
  658.3 16.7 %fusion.220 = f32[12,12]{1,0:T(8,128)S(1)} fusion(bf16[12,512,1024]{2,0,1:T(8,128)(2,1)} %fusion.219, bf16[12,512,1024]{2,1,0:T(8,128)(2,1)} %multiply_convert_fusion.13, f32[12,12]{1,0:T(8,128)S(1)} %copy-done.40, pred[]{:T(512)S(6)} %compare.3), kind=kOutput, calls=%fused_computation.57.clone.1 | convolution fusion | flops 150995232 | bytes 25166976 | tf_op jit(solution)/shard_map/while/body/eval_jaxpr/while/body/eval_jaxpr/hqk,jqk->hj/dot_general | solution.py:176
  675.6 11.6 convert_bitcast_fusion.7
  687.2 16.3 %multiply_convert_fusion.14 = bf16[12,512,64]{1,2,0:T(8,128)(2,1)} fusion(bf16[1024,12,64]{0,2,1:T(8,128)(2,1)} %copy-done.4, bf16[12,512,1024]{2,0,1:T(8,128)(2,1)} %convert_bitcast_fusion.7), kind=kOutput, calls=%fused_computation.53.clone.1 | convolution fusion | flops 806092800 | bytes 14942208 | tf_op jit(solution)/shard_map/while/body/eval_jaxpr/while/body/eval_jaxpr/hqk,khd->qhd/dot_general | solution.py:183
  703.5 16.9 %bitcast_add_fusion.5 = f32[1024,12,64]{0,2,1:T(8,128)} fusion(f32[1024,12,64]{0,2,1:T(8,128)} %get-tuple-element.638, bf16[512,12,64]{0,2,1:T(8,128)(2,1)S(1)} %bitcast.306, bf16[12,512,1024]{2,0,1:T(8,128)(2,1)S(1)} %copy-done.1, pred[]{:T(512)S(6)} %compare.3), kind=kOutput, calls=%fused_computation.50.clone.1 | convolution fusion | flops 807665664 | bytes 19660800 | tf_op jit(solution)/shard_map/while/body/eval_jaxpr/while/body/eval_jaxpr/hqk,qhd->khd/dot_general | solution.py:190
  731.3 8.1 multiply_convert_fusion.13
  739.4 6.4 convolution_convert_fusion.6
  745.8 23.6 %fusion.216 = f32[512,1024,12]{1,2,0:T(8,128)} fusion(bf16[12,512,1024]{2,1,0:T(8,128)(2,1)} %multiply_convert_fusion.13, bf16[12,12]{1,0:T(8,128)(2,1)S(1)} %get-tuple-element.665), kind=kOutput, calls=%fused_computation.38.clone.1 | convolution fusion | flops 150994944 | bytes 37749024 | tf_op jit(solution)/shard_map/while/body/eval_jaxpr/while/body/eval_jaxpr/hqk,hj->jqk/dot_general | solution.py:58
  769.4 19.8 %fusion.221 = bf16[12,512,1024]{2,0,1:T(8,128)(2,1)} fusion(f32[512,1024,12]{1,2,0:T(8,128)} %fusion.216, f32[12,512]{0,1:T(8,128)S(1)} %dynamic-slice_bitcast_fusion.2, pred[512,1024]{1,0:T(8,128)(4,1)S(1)} %fusion.217), kind=kLoop, calls=%fused_computation.31.clone.clone.clone.clone.clone.clone.1.clone.1 | loop fusion | flops 18874368 | bytes 38297600 | tf_op jit(solution)/shard_map/while/body/eval_jaxpr/while/body/eval_jaxpr/jqk,iqk->ji/dot_general | solution.py:170
  789.2 16.9 %fusion.222 = f32[12,12]{1,0:T(8,128)S(1)} fusion(bf16[12,512,1024]{2,1,0:T(8,128)(2,1)} %convolution_convert_fusion.6, f32[12,12]{1,0:T(8,128)S(1)} %copy-done.37, pred[]{:T(512)S(6)} %compare.3, bf16[12,512,1024]{2,0,1:T(8,128)(2,1)} %fusion.221), kind=kOutput, calls=%fused_computation.56.clone.2 | convolution fusion | flops 150995232 | bytes 25166976 | tf_op jit(solution)/shard_map/while/body/eval_jaxpr/while/body/eval_jaxpr/jqk,iqk->ji/dot_general | solution.py:170
  806.1 22.1 %convert_bitcast_fusion.8 = bf16[12,512,1024]{2,0,1:T(8,128)(2,1)} fusion(f32[512,1024,12]{1,2,0:T(8,128)} %fusion.216, f32[12,512]{0,1:T(8,128)S(1)} %dynamic-slice_bitcast_fusion.2, pred[512,1024]{1,0:T(8,128)(4,1)S(1)} %fusion.217, bf16[12,12]{0,1:T(8,128)(2,1)S(1)} %get-tuple-element.669), kind=kOutput, calls=%fused_computation.40.clone.1 | convolution fusion | flops 176160768 | bytes 38297888 | tf_op jit(solution)/shard_map/while/body/eval_jaxpr/while/body/eval_jaxpr/jqk,ji->iqk/dot_general | solution.py:160
  828.3 22.1 %bitcast_add_fusion.6 = f32[1024,12,64]{0,2,1:T(8,128)} fusion(f32[1024,12,64]{0,2,1:T(8,128)} %get-tuple-element.639, bf16[512,12,64]{0,2,1:T(8,128)(2,1)S(1)} %bitcast.308, bf16[12,512,1024]{2,0,1:T(8,128)(2,1)} %convert_bitcast_fusion.8, pred[]{:T(512)S(6)} %compare.3), kind=kOutput, calls=%fused_computation.49.clone.1 | convolution fusion | flops 806879232 | bytes 19660800 | tf_op jit(solution)/shard_map/while/body/eval_jaxpr/while/body/eval_jaxpr/iqk,qid->kid/dot_general | solution.py:195
  850.3 48.7 %fusion.218 = (f32[12,512]{0,1:T(8,128)S(1)}, f32[512,1024,12]{1,2,0:T(8,128)}) fusion(f32[512,1024,12]{1,2,0:T(8,128)} %fusion.216, f32[12,512]{0,1:T(8,128)S(1)} %dynamic-slice_bitcast_fusion.2, pred[512,1024]{1,0:T(8,128)(4,1)S(1)} %fusion.217, bf16[12,12]{0,1:T(8,128)(2,1)S(1)} %get-tuple-element.669, ...), kind=kOutput, calls=%fused_computation.25.clone.1 | convolution fusion | flops 176154624 | bytes 63488288 | tf_op jit(solution)/shard_map/while/body/eval_jaxpr/while/body/eval_jaxpr/iqk,ji->jqk/dot_general | solution.py:167
  899.0 27.7 %fusion.219 = bf16[12,512,1024]{2,0,1:T(8,128)(2,1)} fusion(f32[512,1024,12]{1,2,0:T(8,128)} %get-tuple-element.578, f32[512,1024,12]{1,2,0:T(8,128)} %fusion.216, f32[12,512]{0,1:T(8,128)S(1)} %get-tuple-element.579, f32[12,512]{0,1:T(8,128)S(1)} %dynamic-slice_bitcast_fusion.2, pred[512,1024]{1,0:T(8,128)(4,1)S(1)} %fusion.217), kind=kLoop, calls=%fused_computation.27.clone.1 | loop fusion | flops 31457280 | bytes 63488000 | tf_op jit(solution)/shard_map/while/body/eval_jaxpr/while/body/eval_jaxpr/convert_element_type | solution.py:175
  926.7 16.7 %fusion.220 = f32[12,12]{1,0:T(8,128)S(1)} fusion(bf16[12,512,1024]{2,0,1:T(8,128)(2,1)} %fusion.219, bf16[12,512,1024]{2,1,0:T(8,128)(2,1)} %multiply_convert_fusion.13, f32[12,12]{1,0:T(8,128)S(1)} %copy-done.40, pred[]{:T(512)S(6)} %compare.3), kind=kOutput, calls=%fused_computation.57.clone.1 | convolution fusion | flops 150995232 | bytes 25166976 | tf_op jit(solution)/shard_map/while/body/eval_jaxpr/while/body/eval_jaxpr/hqk,jqk->hj/dot_general | solution.py:176
  944.0 11.6 convert_bitcast_fusion.7
  955.7 16.3 %multiply_convert_fusion.14 = bf16[12,512,64]{1,2,0:T(8,128)(2,1)} fusion(bf16[1024,12,64]{0,2,1:T(8,128)(2,1)} %copy-done.4, bf16[12,512,1024]{2,0,1:T(8,128)(2,1)} %convert_bitcast_fusion.7), kind=kOutput, calls=%fused_computation.53.clone.1 | convolution fusion | flops 806092800 | bytes 14942208 | tf_op jit(solution)/shard_map/while/body/eval_jaxpr/while/body/eval_jaxpr/hqk,khd->qhd/dot_general | solution.py:183
  972.0 18.2 %bitcast_add_fusion.5 = f32[1024,12,64]{0,2,1:T(8,128)} fusion(f32[1024,12,64]{0,2,1:T(8,128)} %get-tuple-element.638, bf16[512,12,64]{0,2,1:T(8,128)(2,1)S(1)} %bitcast.306, bf16[12,512,1024]{2,0,1:T(8,128)(2,1)S(1)} %copy-done.1, pred[]{:T(512)S(6)} %compare.3), kind=kOutput, calls=%fused_computation.50.clone.1 | convolution fusion | flops 807665664 | bytes 19660800 | tf_op jit(solution)/shard_map/while/body/eval_jaxpr/while/body/eval_jaxpr/hqk,qhd->khd/dot_general | solution.py:190
  1002.2 5.5 copy.104
  1007.7 11.2 reduce.4
  1020.7 4.6 all-to-all-start.6
  1025.4 12.5 fusion.113
  1038.2 5.5 copy.105
  1043.7 11.2 reduce.2
  1061.2 11.0 fusion.111
  1076.2 11.2 reduce.3
  1093.1 5.7 fusion.97
  1107.8 5.4 fusion.86
  1118.8 5.2 fusion.93
  1124.1 13.3 add_convert_fusion
  1146.1 44.0 %all-reduce = (f32[768]{0:T(1024)}, f32[12,12]{1,0:T(8,128)}, f32[12,12]{1,0:T(8,128)}, f32[768]{0:T(1024)}) all-reduce(f32[768]{0:T(1024)S(1)} %get-tuple-element.348, f32[12,12]{1,0:T(8,128)S(1)} %copy-done.42, f32[12,12]{1,0:T(8,128)S(1)} %copy-done.39, f32[768]{0:T(1024)S(1)} %copy-done.46), channel_id=1, replica_groups=mesh['rows'=8,'seq'=4] {'rows','seq'}, use_global_device_ids=true, to_apply=%region_12.13 | all-reduce | flops 1824 | bytes 14592 | tf_op jit(solution)/shard_map/psum | solution.py:251
  1190.2 5.1 fusion.79
  1195.2 367.6 %all-reduce.4.cloned.1.call-done = (f32[768,768]{1,0:T(8,128)}, f32[768,768]{1,0:T(8,128)}, f32[768,768]{1,0:T(8,128)}, f32[768,768]{1,0:T(8,128)}, f32[768,3072]{1,0:T(8,128)}, /*index=5*/f32[3072,768]{1,0:T(8,128)}) async-done(((f32[768,768]{1,0:T(8,128)}, f32[768,768]{1,0:T(8,128)}, f32[768,768]{1,0:T(8,128)}, f32[768,768]{1,0:T(8,128)}, f32[768,3072]{1,0:T(8,128)}, /*index=5*/f32[3072,768]{1,0:T(8,128)}), ...) | async-done | bytes 28311568 | tf_op jit(solution)/shard_map/psum | solution.py:251
  1572.7 9.3 copy.265
  (249 shorter events, 161.6 us)
Async XLA Ops:
  7.2 4.4 copy-start
  9.7 4.4 copy-start.32
  14.1 24.3 %all-to-all-start.2 = ((bf16[4,256,768]{2,1,0:T(8,128)(2,1)}), bf16[4,256,768]{2,1,0:T(8,128)(2,1)S(1)}, u32[]{:S(2)}, u32[]{:S(2)}) async-start(bf16[4,256,768]{2,1,0:T(8,128)(2,1)} %bitcast.337), calls=%async_computation.2 | async-start | bytes 3145728 | tf_op jit(solution)/shard_map/all_to_all | solution.py:96
  38.4 24.5 %all-to-all-start.1 = ((bf16[4,256,768]{2,1,0:T(8,128)(2,1)}), bf16[4,256,768]{2,1,0:T(8,128)(2,1)}, u32[]{:S(2)}, u32[]{:S(2)}) async-start(bf16[4,256,768]{2,1,0:T(8,128)(2,1)} %bitcast.336), calls=%async_computation.1 | async-start | bytes 3145728 | tf_op jit(solution)/shard_map/all_to_all | solution.py:95
  47.0 20.2 %copy-start.45 = (bf16[12,12]{1,0:T(8,128)(2,1)S(1)}, bf16[12,12]{1,0:T(8,128)(2,1)}, u32[]{:S(2)}) copy-start(bf16[12,12]{1,0:T(8,128)(2,1)} %param.25) | copy-start | bytes 868
  47.0 20.3 %copy-start.26 = (bf16[12,12]{1,0:T(8,128)(2,1)S(1)}, bf16[12,12]{1,0:T(8,128)(2,1)}, u32[]{:S(2)}) copy-start(bf16[12,12]{1,0:T(8,128)(2,1)} %param.24) | copy-start | bytes 868
  62.9 24.5 %all-to-all-start = ((bf16[4,256,768]{2,1,0:T(8,128)(2,1)}), bf16[4,256,768]{2,1,0:T(8,128)(2,1)}, u32[]{:S(2)}, u32[]{:S(2)}) async-start(bf16[4,256,768]{2,1,0:T(8,128)(2,1)} %bitcast.334), calls=%async_computation | async-start | bytes 3145728 | tf_op jit(solution)/shard_map/all_to_all | solution.py:94
  159.2 16.1 %copy-start.7 = (f32[12,512]{0,1:T(8,128)}, f32[12,512]{0,1:T(8,128)S(1)}, u32[]{:S(2)}) copy-start(f32[12,512]{0,1:T(8,128)S(1)} %get-tuple-element.562) | copy-start | bytes 73732 | tf_op jit(solution)/shard_map/while/body/eval_jaxpr/while
  268.0 16.1 %copy-start.7 = (f32[12,512]{0,1:T(8,128)}, f32[12,512]{0,1:T(8,128)S(1)}, u32[]{:S(2)}) copy-start(f32[12,512]{0,1:T(8,128)S(1)} %get-tuple-element.562) | copy-start | bytes 73732 | tf_op jit(solution)/shard_map/while/body/eval_jaxpr/while
  334.2 18.4 %copy-start.28 = (bf16[12,12]{0,1:T(8,128)(2,1)}, bf16[12,12]{0,1:T(8,128)(2,1)S(1)}, u32[]{:S(2)}) copy-start(bf16[12,12]{0,1:T(8,128)(2,1)S(1)} %get-tuple-element.725) | copy-start | bytes 868
  385.7 4.4 copy-start.43
  385.7 16.2 %slice-start.5 = ((s8[4718592]{0:T(1024)(128)(4,1)}), s8[4194304]{0:T(1024)(128)(4,1)S(1)}, s32[]{:S(2)}) async-start(s8[4718592]{0:T(1024)(128)(4,1)} %bitcast.346), calls=%async_computation.14 | async-start | bytes 8388608
  390.1 35.6 %copy-start.16 = (f32[1024,768]{1,0:T(8,128)}, f32[1024,768]{1,0:T(8,128)S(1)}, u32[]{:S(2)}) copy-start(f32[1024,768]{1,0:T(8,128)S(1)} %get-tuple-element.417) | copy-start | bytes 9437188
  390.1 35.6 %copy-start.35 = (f32[1024]{0:T(1024)}, f32[1024]{0:T(1024)S(1)}, u32[]{:S(2)}) copy-start(f32[1024]{0:T(1024)S(1)} %add_rsqrt_fusion) | copy-start | bytes 12292
  390.1 11.7 copy-start.22
  390.2 11.7 slice-start.6
  390.2 27.2 %slice-start.3 = ((s8[4718592]{0:T(1024)(128)(4,1)}), s8[4194304]{0:T(1024)(128)(4,1)S(1)}, s32[]{:S(2)}) async-start(s8[4718592]{0:T(1024)(128)(4,1)} %bitcast.344), calls=%async_computation.12 | async-start | bytes 8388608
  401.9 15.4 slice-start.4
  427.0 2.6 copy-start.10
  429.6 4.6 copy-start.30
  429.6 4.6 copy-start.34
  429.6 24.6 %all-to-all-start.4 = ((bf16[4,256,768]{2,1,0:T(8,128)(2,1)}), bf16[4,256,768]{2,1,0:T(8,128)(2,1)}, u32[]{:S(2)}, u32[]{:S(2)}) async-start(bf16[4,256,768]{2,1,0:T(8,128)(2,1)} %bitcast.335), calls=%async_computation.4 | async-start | bytes 3145728 | tf_op jit(solution)/shard_map/all_to_all | solution.py:145
  434.1 21.4 %copy-start.27 = (bf16[12,12]{1,0:T(8,128)(2,1)S(1)}, bf16[12,12]{1,0:T(8,128)(2,1)}, u32[]{:S(2)}) copy-start(bf16[12,12]{1,0:T(8,128)(2,1)} %param.24) | copy-start | bytes 868
  434.1 21.4 %copy-start.29 = (bf16[12,12]{0,1:T(8,128)(2,1)S(1)}, bf16[12,12]{0,1:T(8,128)(2,1)}, u32[]{:S(2)}) copy-start(bf16[12,12]{0,1:T(8,128)(2,1)} %copy-done.28) | copy-start | bytes 868
  455.6 3.3 copy-start.4
  455.6 16.2 %copy-start.24 = (s32[1024]{0:T(1024)}, s32[1024]{0:T(1024)S(1)}, u32[]{:S(2)}) copy-start(s32[1024]{0:T(1024)S(1)} %get-tuple-element.663) | copy-start | bytes 12292 | tf_op jit(solution)/shard_map/while/body/eval_jaxpr/while
  455.7 16.2 %copy-start.50 = (s32[2]{0:T(128)}, s32[2]{0:T(128)S(1)}, u32[]{:S(2)}) copy-start(s32[2]{0:T(128)S(1)} %get-tuple-element.661) | copy-start | bytes 28 | tf_op jit(solution)/shard_map/while/body/eval_jaxpr/while
  463.7 8.1 copy-start.2
  463.7 8.1 copy-start.8
  501.8 20.1 %copy-start.37 = (f32[12,12]{1,0:T(8,128)S(1)}, f32[12,12]{1,0:T(8,128)}, u32[]{:S(2)}) copy-start(f32[12,12]{1,0:T(8,128)} %get-tuple-element.641) | copy-start | bytes 1732 | tf_op jit(solution)/shard_map/while/body/eval_jaxpr/while
  538.8 21.9 %copy-start.38 = (f32[12,12]{1,0:T(8,128)}, f32[12,12]{1,0:T(8,128)S(1)}, u32[]{:S(2)}) copy-start(f32[12,12]{1,0:T(8,128)S(1)} %fusion.222) | copy-start | bytes 1732 | tf_op jit(solution)/shard_map/while/body/eval_jaxpr/while
  630.6 27.7 %copy-start.40 = (f32[12,12]{1,0:T(8,128)S(1)}, f32[12,12]{1,0:T(8,128)}, u32[]{:S(2)}) copy-start(f32[12,12]{1,0:T(8,128)} %get-tuple-element.640) | copy-start | bytes 1732 | tf_op jit(solution)/shard_map/while/body/eval_jaxpr/while
  687.2 16.3 %copy-start.1 = (bf16[12,512,1024]{2,0,1:T(8,128)(2,1)S(1)}, bf16[12,512,1024]{2,0,1:T(8,128)(2,1)}, u32[]{:S(2)}) copy-start(bf16[12,512,1024]{2,0,1:T(8,128)(2,1)} %convert_bitcast_fusion.7) | copy-start | bytes 37748740 | tf_op jit(solution)/shard_map/while/body/eval_jaxpr/while
  687.2 16.3 %copy-start.3 = (bf16[512,768]{0,1:T(8,128)(2,1)S(1)}, bf16[512,768]{0,1:T(8,128)(2,1)}, u32[]{:S(2)}) copy-start(bf16[512,768]{0,1:T(8,128)(2,1)} %copy-done.2) | copy-start | bytes 2359300 | tf_op jit(solution)/shard_map/while/body/eval_jaxpr/while
  723.3 3.3 copy-start.4
  723.3 16.1 %copy-start.24 = (s32[1024]{0:T(1024)}, s32[1024]{0:T(1024)S(1)}, u32[]{:S(2)}) copy-start(s32[1024]{0:T(1024)S(1)} %get-tuple-element.663) | copy-start | bytes 12292 | tf_op jit(solution)/shard_map/while/body/eval_jaxpr/while
  723.3 16.1 %copy-start.50 = (s32[2]{0:T(128)}, s32[2]{0:T(128)S(1)}, u32[]{:S(2)}) copy-start(s32[2]{0:T(128)S(1)} %get-tuple-element.661) | copy-start | bytes 28 | tf_op jit(solution)/shard_map/while/body/eval_jaxpr/while
  731.2 8.1 copy-start.2
  731.3 8.1 copy-start.8
  769.4 19.8 %copy-start.37 = (f32[12,12]{1,0:T(8,128)S(1)}, f32[12,12]{1,0:T(8,128)}, u32[]{:S(2)}) copy-start(f32[12,12]{1,0:T(8,128)} %get-tuple-element.641) | copy-start | bytes 1732 | tf_op jit(solution)/shard_map/while/body/eval_jaxpr/while
  806.1 22.1 %copy-start.38 = (f32[12,12]{1,0:T(8,128)}, f32[12,12]{1,0:T(8,128)S(1)}, u32[]{:S(2)}) copy-start(f32[12,12]{1,0:T(8,128)S(1)} %fusion.222) | copy-start | bytes 1732 | tf_op jit(solution)/shard_map/while/body/eval_jaxpr/while
  899.0 27.7 %copy-start.40 = (f32[12,12]{1,0:T(8,128)S(1)}, f32[12,12]{1,0:T(8,128)}, u32[]{:S(2)}) copy-start(f32[12,12]{1,0:T(8,128)} %get-tuple-element.640) | copy-start | bytes 1732 | tf_op jit(solution)/shard_map/while/body/eval_jaxpr/while
  955.7 16.3 %copy-start.1 = (bf16[12,512,1024]{2,0,1:T(8,128)(2,1)S(1)}, bf16[12,512,1024]{2,0,1:T(8,128)(2,1)}, u32[]{:S(2)}) copy-start(bf16[12,512,1024]{2,0,1:T(8,128)(2,1)} %convert_bitcast_fusion.7) | copy-start | bytes 37748740 | tf_op jit(solution)/shard_map/while/body/eval_jaxpr/while
  955.7 16.3 %copy-start.3 = (bf16[512,768]{0,1:T(8,128)(2,1)S(1)}, bf16[512,768]{0,1:T(8,128)(2,1)}, u32[]{:S(2)}) copy-start(bf16[512,768]{0,1:T(8,128)(2,1)} %copy-done.2) | copy-start | bytes 2359300 | tf_op jit(solution)/shard_map/while/body/eval_jaxpr/while
  1020.7 4.7 copy-start.23
  1020.7 36.0 %all-to-all-start.6 = ((bf16[4,2,98304]{2,1,0:T(2,128)(2,1)}), bf16[4,2,98304]{2,1,0:T(2,128)(2,1)}, u32[]{:S(2)}, u32[]{:S(2)}) async-start(bf16[4,2,98304]{2,1,0:T(2,128)(2,1)} %reshape.358), calls=%async_computation.6 | async-start | bytes 3145728 | tf_op jit(solution)/shard_map/all_to_all | solution.py:226
  1025.4 12.5 copy-start.6
  1054.9 6.2 copy-start.36
  1054.9 6.2 copy-start.44
  1056.8 32.5 %all-to-all-start.7 = ((bf16[4,2,98304]{2,1,0:T(2,128)(2,1)}), bf16[4,2,98304]{2,1,0:T(2,128)(2,1)}, u32[]{:S(2)}, u32[]{:S(2)}) async-start(bf16[4,2,98304]{2,1,0:T(2,128)(2,1)} %reshape.360), calls=%async_computation.7 | async-start | bytes 3145728 | tf_op jit(solution)/shard_map/all_to_all | solution.py:227
  1061.1 11.0 copy-start.12
  1089.3 26.7 %all-to-all-start.5 = ((bf16[4,2,98304]{2,1,0:T(2,128)(2,1)}), bf16[4,2,98304]{2,1,0:T(2,128)(2,1)S(1)}, u32[]{:S(2)}, u32[]{:S(2)}) async-start(bf16[4,2,98304]{2,1,0:T(2,128)(2,1)} %reshape.356), calls=%async_computation.5 | async-start | bytes 3145728 | tf_op jit(solution)/shard_map/all_to_all | solution.py:225
  1092.9 470.0 %all-reduce.4.cloned.1.call-start = ((), (), s32[]{:S(2)}) async-start(), calls=%async_computation.8 | async-start | bytes 56623104 | tf_op jit(solution)/shard_map/psum | solution.py:251
  1107.8 5.4 copy-start.13
  1107.8 5.4 copy-start.20
  1124.0 13.3 copy-start.14
  1124.0 13.3 copy-start.48
  1142.2 3.9 copy-start.39
  1142.2 3.9 copy-start.42
  1142.3 3.9 copy-start.46
  1562.9 3.4 copy-start.19
  1571.3 10.7 slice-start
  1572.7 9.3 slice-start.1
  1572.7 9.3 slice-start.2
  (18 other events, 38.2 us)
Sparse Core Ops, SparseCore 0:
  1124.2 438.6 all-reduce.3
where the time goes:
time: 1600 us; the launch traced here: 1590 us
  matrix products  702 us (44%)
  waiting for transfers between devices  423 us (26%)
  other arithmetic  198 us (12%)
  local copies, waits for them, and re-layouts  115 us (7%)
  blocking collectives  68.9 us (4%)
  loops' own time  41.3 us (3%)
  starting transfers between devices  30.2 us (2%)
    psum x1, waiting for transfers between devices, per_device(): lax.psum((grad_gain_one, grad_w_query, grad_w_key, grad_w_value, grad_w_o...  368 us
    dot_general x4, matrix products, block_scores(): jnp.einsum('hqk,hj->jqk', scores, mix_logits, preferred_element_type=jnp....  126 us
    dot_general x2, matrix products, block_step(): jnp.einsum('iqk,ji->jqk', grad_blended, mix_weights, preferred_element_ty...  97.4 us
    convert_element_type x2, other arithmetic, block_step(): grad_logits = (softmax * (grad_soft - jnp.sum(softmax * grad_soft, axis=-...  55.4 us
    unnamed x104, local copies, waits for them, and re-layouts  51.2 us
    unnamed x11, other arithmetic  46 us
    dot_general x2, matrix products, one_block(): jnp.einsum('jqk,ji->iqk', soft_low, mix_weights, preferred_element_type=j...  45.5 us
    psum x1, blocking collectives, per_device(): lax.psum((grad_gain_one, grad_w_query, grad_w_key, grad_w_value, grad_w_o...  44 us
  transfers between devices with their start and end apart: 8, of which 5 were waited for; matrix products, arithmetic and copies ran while one was open for 8% of the time, Pallas kernels for 0%

commit v1 on v0

v1 whole, which is shorter than its diff:
```python
from functools import partial

import jax
import jax.numpy as jnp
from jax import lax
from jax.experimental import pallas as pl
from jax.experimental.pallas import tpu as pltpu
from jax.sharding import PartitionSpec as P

D, H, DH, LEN, TILE = 768, 12, 64, 1024, 256
TILES = LEN // TILE
F32, BF16 = jnp.float32, jnp.bfloat16
HEADS_PER_STEP = 1
VMEM_LIMIT = 60 * 1024 * 1024


def span(i):
    return slice(i * TILE, (i + 1) * TILE)


def head_rows(h):
    return slice(h * DH, (h + 1) * DH)


def mm(a, b):
    return jnp.dot(a, b, preferred_element_type=F32)


def scale_rows(dst, src, weights, pick):
    for h in range(H):
        w = pick(weights, h)
        dst[head_rows(h), :] = (src[head_rows(h), :].astype(F32) * w).astype(BF16)


def soft_kernel(mix, id_row, id_col, q_t, k, soft, bias, scaled):
    j = pl.program_id(0)

    @pl.when(j == 0)
    def build_bias():
        for t in range(TILES):
            for u in range(t + 1):
                allowed = id_col[span(u), :] == id_row[:, span(t)]
                if u == t:
                    key = lax.broadcasted_iota(jnp.int32, (TILE, TILE), 0)
                    query = lax.broadcasted_iota(jnp.int32, (TILE, TILE), 1)
                    allowed = allowed & (key <= query)
                bias[span(u), span(t)] = jnp.where(allowed, 0.0, -1e30)

    scale_rows(scaled, q_t, mix, lambda w, h: w[h, j])
    for t in range(TILES):
        n = (t + 1) * TILE
        logits = mm(k[:n, :], scaled[:, span(t)]) + bias[:n, span(t)]
        top = jnp.max(logits, axis=0, keepdims=True)
        e = jnp.exp(logits - top)
        inv = 1.0 / jnp.sum(e, axis=0, keepdims=True)
        soft[0, :n, span(t)] = (e * inv).astype(BF16)


def attend_kernel(mix, soft, v_t, out, acc):
    j = pl.program_id(0)

    @pl.when(j == 0)
    def zero():
        acc[...] = jnp.zeros_like(acc)

    for t in range(TILES):
        n = (t + 1) * TILE
        part = mm(v_t[:, :n], soft[0, :n, span(t)])
        for h in range(H):
            acc[head_rows(h), span(t)] += part[head_rows(h), :] * mix[j, h]

    @pl.when(j == H - 1)
    def finish():
        for t in range(TILES):
            out[span(t), :] = acc[:, span(t)].T.astype(BF16)


def values_kernel(mix_row, soft, v, g, out, mix_grad, acc):
    j = pl.program_id(0)

    @pl.when(j == 0)
    def zero():
        acc[...] = jnp.zeros_like(acc)

    w = mix_row[0]
    total = jnp.zeros((1, D), F32)
    for u in range(TILES):
        part = mm(soft[0, span(u), u * TILE:], g[u * TILE:, :])
        acc[span(u), :] += part * w
        total = total + jnp.sum(part * v[span(u), :].astype(F32), axis=0, keepdims=True)
    mix_grad[0] = total

    @pl.when(j == H - 1)
    def finish():
        out[...] = acc[...].astype(BF16)


def queries_kernel(mix_w, mix_l, soft, v, g_t, k_t, q_t, out, grad_logits, mix_grad, acc, scaled):
    j = pl.program_id(0)

    @pl.when(j == 0)
    def zero():
        acc[...] = jnp.zeros_like(acc)

    scale_rows(scaled, g_t, mix_w, lambda w, h: w[j, h])
    total = jnp.zeros((D, 128), F32)
    for t in range(TILES):
        n = (t + 1) * TILE
        grad_soft = mm(v[:n, :], scaled[:, span(t)])
        p = soft[0, :n, span(t)].astype(F32)
        weighted = p * grad_soft
        dots = jnp.sum(weighted, axis=0, keepdims=True)
        gl = (weighted - p * dots).astype(BF16)
        grad_logits[0, :n, span(t)] = gl
        part = mm(k_t[:, :n], gl)
        for h in range(H):
            acc[head_rows(h), span(t)] += part[head_rows(h), :] * mix_l[h, j]
        prod = part * q_t[:, span(t)].astype(F32)
        total = total + prod[:, :128] + prod[:, 128:]
    mix_grad[0] = jnp.sum(total, axis=1, keepdims=True)

    @pl.when(j == H - 1)
    def finish():
        for t in range(TILES):
            out[span(t), :] = acc[:, span(t)].T.astype(BF16)


def keys_kernel(mix_row, grad_logits, q, out, acc):
    j = pl.program_id(0)

    @pl.when(j == 0)
    def zero():
        acc[...] = jnp.zeros_like(acc)

    w = mix_row[0]
    for u in range(TILES):
        acc[span(u), :] += mm(grad_logits[0, span(u), u * TILE:], q[u * TILE:, :]) * w

    @pl.when(j == H - 1)
    def finish():
        out[...] = acc[...].astype(BF16)


def whole(shape):
    return pl.BlockSpec(shape, lambda j: (0,) * len(shape), pipeline_mode=pl.Buffered(1))


def per_head(shape):
    return pl.BlockSpec((1,) + shape, lambda j: (j,) + (0,) * len(shape))


SMEM = pl.BlockSpec(memory_space=pltpu.SMEM)


def params():
    return pltpu.CompilerParams(dimension_semantics=("arbitrary",), vmem_limit_bytes=VMEM_LIMIT)


def call(kernel, in_specs, out_specs, out_shape, scratch, name):
    return pl.pallas_call(
        kernel, grid=(H,), in_specs=in_specs, out_specs=out_specs, out_shape=out_shape,
        scratch_shapes=scratch, compiler_params=params(), name=name)


def shape(s, t=BF16):
    return jax.ShapeDtypeStruct(s, t)


def softmaxes(mix, ids, q_t, k):
    return call(
        soft_kernel,
        [SMEM, whole((1, LEN)), whole((LEN, 1)), whole((D, LEN)), whole((LEN, D))],
        per_head((LEN, LEN)), shape((H, LEN, LEN)),
        [pltpu.VMEM((LEN, LEN), F32), pltpu.VMEM((D, LEN), BF16)], "softmaxes",
    )(mix, ids.reshape(1, LEN), ids.reshape(LEN, 1), q_t, k)


def attend(mix, soft, v_t):
    return call(
        attend_kernel, [SMEM, per_head((LEN, LEN)), whole((D, LEN))], whole((LEN, D)), shape((LEN, D)),
        [pltpu.VMEM((D, LEN), F32)], "attend")(mix, soft, v_t)


def value_grads(mix_rows, soft, v, g):
    return call(
        values_kernel, [per_head((1, D)), per_head((LEN, LEN)), whole((LEN, D)), whole((LEN, D))],
        [whole((LEN, D)), per_head((1, D))], [shape((LEN, D)), shape((H, 1, D), F32)],
        [pltpu.VMEM((LEN, D), F32)], "value_grads")(mix_rows, soft, v, g)


def query_grads(mix_w, mix_l, soft, v, g_t, k_t, q_t):
    return call(
        queries_kernel,
        [SMEM, SMEM, per_head((LEN, LEN)), whole((LEN, D)), whole((D, LEN)), whole((D, LEN)), whole((D, LEN))],
        [whole((LEN, D)), per_head((LEN, LEN)), per_head((D, 1))],
        [shape((LEN, D)), shape((H, LEN, LEN)), shape((H, D, 1), F32)],
        [pltpu.VMEM((D, LEN), F32), pltpu.VMEM((D, LEN), BF16)], "query_grads",
    )(mix_w, mix_l, soft, v, g_t, k_t, q_t)


def key_grads(mix_rows, grad_logits, q):
    return call(
        keys_kernel, [per_head((1, D)), per_head((LEN, LEN)), whole((LEN, D))], whole((LEN, D)), shape((LEN, D)),
        [pltpu.VMEM((LEN, D), F32)], "key_grads")(mix_rows, grad_logits, q)


epsilon = 1e-06


def cross_rows(left, right):
    return lax.dot_general(left, right, (((0,), (0,)), ((), ())), preferred_element_type=F32)


def against(left, right):
    return lax.dot_general(left, right, (((1,), (1,)), ((), ())), preferred_element_type=F32)


def norm_parts(values, gain):
    inverse = lax.rsqrt(jnp.mean(values * values, axis=-1, keepdims=True) + epsilon)
    return (values * inverse * gain, inverse)


def norm_back(values, inverse, gain, upstream):
    weighted = upstream * gain
    grad_gain = jnp.sum(upstream * values * inverse, axis=0)
    grad_values = inverse * weighted - values * inverse * inverse * inverse * jnp.mean(
        weighted * values, axis=-1, keepdims=True
    )
    return (grad_values, grad_gain)


def to_rows(values):
    return lax.all_to_all(values, "seq", split_axis=0, concat_axis=1, tiled=True).reshape(LEN, D)


def to_tokens(values):
    return lax.all_to_all(values.reshape(1, LEN, D), "seq", split_axis=1, concat_axis=0, tiled=True)


def per_device(
    inputs,
    segment_ids,
    gain_one,
    w_query,
    w_key,
    w_value,
    w_out,
    mix_logits,
    mix_weights,
    gain_two,
    w_hidden,
    w_back,
    cotangent,
):
    ids = lax.dynamic_slice_in_dim(segment_ids, lax.axis_index("seq"), 1, 0)
    x_row = to_rows(inputs)
    cot = to_rows(cotangent)
    x = x_row.astype(F32)
    normed_f, inverse_one = norm_parts(x, gain_one)
    normed = normed_f.astype(BF16)
    q = mm(normed, w_query).astype(BF16)
    k = mm(normed, w_key).astype(BF16)
    v = mm(normed, w_value).astype(BF16)
    scale = DH ** -0.5
    ml = mix_logits.astype(F32) * scale
    mw = mix_weights.astype(F32)
    ml_rows = jnp.repeat(ml.T, DH, axis=1)[:, None, :]
    mw_rows = jnp.repeat(mw, DH, axis=1)[:, None, :]
    q_t = q.T
    soft = softmaxes(ml, ids, q_t, k)
    attended = attend(mw, soft, v.T)
    middle = x + mm(attended, w_out)
    normed_two_f, inverse_two = norm_parts(middle, gain_two)
    normed_two = normed_two_f.astype(BF16)
    hidden = mm(normed_two, w_hidden)
    activated = jax.nn.gelu(hidden, approximate=True).astype(BF16)
    block_out = to_tokens((middle + mm(activated, w_back)).astype(BF16))
    grad_w_back = cross_rows(activated, cot)
    grad_act = against(cot, w_back)
    unused, gelu_pull = jax.vjp(partial(jax.nn.gelu, approximate=True), hidden)
    grad_hidden = gelu_pull(grad_act)[0].astype(BF16)
    grad_w_hidden = cross_rows(normed_two, grad_hidden)
    grad_n2 = against(grad_hidden, w_hidden)
    grad_middle_norm, grad_gain_two = norm_back(middle, inverse_two, gain_two, grad_n2)
    grad_middle = cot.astype(F32) + grad_middle_norm
    grad_attn = grad_middle.astype(BF16)
    grad_w_out = cross_rows(attended, grad_attn)
    grad_attended = against(grad_attn, w_out).astype(BF16)
    gv, mw_parts = value_grads(mw_rows, soft, v, grad_attended)
    gq, grad_logits, ml_parts = query_grads(mw, ml, soft, v, grad_attended.T, k.T, q_t)
    gk = key_grads(ml_rows, grad_logits, q)
    grad_mix_weights = mw_parts.reshape(H, H, DH).sum(-1)
    grad_mix_logits = ml_parts.reshape(H, H, DH).sum(-1).T * scale
    grad_w_query = cross_rows(normed, gq)
    grad_w_key = cross_rows(normed, gk)
    grad_w_value = cross_rows(normed, gv)
    grad_normed = against(gq, w_query) + against(gk, w_key) + against(gv, w_value)
    grad_in_norm, grad_gain_one = norm_back(x, inverse_one, gain_one, grad_normed)
    grad_inputs = to_tokens((grad_middle + grad_in_norm).astype(BF16))
    grads = lax.psum(
        (
            grad_gain_one,
            grad_w_query,
            grad_w_key,
            grad_w_value,
            grad_w_out,
            grad_mix_logits,
            grad_mix_weights,
            grad_gain_two,
            grad_w_hidden,
            grad_w_back,
        ),
        ("rows", "seq"),
    )
    return (block_out, grad_inputs) + tuple(grads)


def solution(mesh):
    sharded, copied = P("rows", "seq", None), P()
    in_specs = (sharded, P("rows", None)) + (copied,) * 10 + (sharded,)
    out_specs = (sharded, sharded) + (copied,) * 10
    return jax.shard_map(
        per_device, mesh=mesh, in_specs=in_specs, out_specs=out_specs, check_vma=False
    )
```

time: 1600 us -> 769 us (0.48)
  matrix products: 702 us -> 94.5 us
  other arithmetic: 198 us -> 32.4 us
  Pallas kernels: 0 us -> 139 us
  waiting for transfers between devices: 423 us -> 310 us
  local copies, waits for them, and re-layouts: 115 us -> 72.2 us
  loops' own time: 41.3 us -> 0 us
  starting transfers between devices: 30.2 us -> 12.5 us
    dot_general x36 -> x6, matrix products: 626 us -> 29.8 us  [mm(): return jnp.dot(a, b, preferred_element_type=F32)]
    pallas_call x0 -> x5, Pallas kernels: none -> 139 us  [the longest x1 50.7 us: query_grads(): call(queries_kernel, [SMEM, SMEM, per_head((LEN, LEN)), whole((LEN, D)),...]
    psum x1, waiting for transfers between devices: 368 us -> 295 us  [per_device(): lax.psum((grad_gain_one, grad_w_query, grad_w_key, grad_w_value, grad_w_o...]
    convert_element_type x7 -> x2, other arithmetic: 67.7 us -> 2.81 us  [the longest x1 2.21 us: per_device(): normed = normed_f.astype(BF16)]
    another operation x2 -> x0, loops' own time: 41.3 us -> none  [the longest x1 29.1 us: forward_row(): block_outs, log_totals = lax.map(one_block, offsets)]
    all_to_all x7 -> x3, waiting for transfers between devices: 55.3 us -> 15.1 us  [the longest x1 15.1 us: to_rows(): lax.all_to_all(values, 'seq', split_axis=0, concat_axis=1, tiled=True)]
    dot_general x2 -> x0, other arithmetic: 39.9 us -> none  [block_step(): jnp.einsum('jqk,iqk->ji', soft_low, grad_blended, preferred_element_type=...]
    reduce_sum x2, other arithmetic: 32.3 us -> 0.2 us  [the longest x1 0.1 us: per_device(): grad_mix_logits = ml_parts.reshape(H, H, DH).sum(-1).T * scale]
  transfers between devices with their start and end apart: 8 -> 4, of which waited for: 5 -> 2; matrix products, arithmetic and copies ran while one was open for 8% -> 11% of each run, Pallas kernels for 0% -> 0%
where the time goes in v1:
time: 769 us; the launch traced here: 758 us
  waiting for transfers between devices  310 us (40%)
  Pallas kernels  139 us (18%)
  matrix products  94.5 us (12%)
  blocking collectives  83 us (11%)
  local copies, waits for them, and re-layouts  72.2 us (9%)
  other arithmetic  32.4 us (4%)
  between operations  14.7 us (2%)
  starting transfers between devices  12.5 us (2%)
    psum x1, waiting for transfers between devices, per_device(): lax.psum((grad_gain_one, grad_w_query, grad_w_key, grad_w_value, grad_w_o...  295 us
    psum x1, blocking collectives, per_device(): lax.psum((grad_gain_one, grad_w_query, grad_w_key, grad_w_value, grad_w_o...  58.6 us
    pallas_call x1, Pallas kernels, query_grads(): call(queries_kernel, [SMEM, SMEM, per_head((LEN, LEN)), whole((LEN, D)),...  50.7 us
    unnamed x91, local copies, waits for them, and re-layouts  43.6 us
    dot_general x6, matrix products, against(): lax.dot_general(left, right, (((1,), (1,)), ((), ())), preferred_element_...  32.6 us
    dot_general x6, matrix products, cross_rows(): lax.dot_general(left, right, (((0,), (0,)), ((), ())), preferred_element_...  32 us
    dot_general x6, matrix products, mm(): return jnp.dot(a, b, preferred_element_type=F32)  29.8 us
    pallas_call x1, Pallas kernels, softmaxes(): call(soft_kernel, [SMEM, whole((1, LEN)), whole((LEN, 1)), whole((D, LEN)...  25.8 us
  transfers between devices with their start and end apart: 4, of which 2 were waited for; matrix products, arithmetic and copies ran while one was open for 11% of the time, Pallas kernels for 0%

profile of v1, /device:TPU:0, one launch (start us, length us, event | category | flops | bytes accessed | tf_op | source)
XLA Modules:
  0.0 757.9 jit_solution(4827272596810745594)
XLA Ops:
  7.2 24.4 %all_to_all.42 = bf16[4,256,768]{2,1,0:T(8,128)(2,1)S(1)} all-to-all(bf16[4,256,768]{2,1,0:T(8,128)(2,1)} %param.13), channel_id=1, replica_groups=mesh['rows'=8,'seq'=4] {'seq'}, dimensions={0} | all-to-all | bytes 3145728 | tf_op jit(solution)/shard_map/all_to_all | solution.py:233
  31.7 4.3 all-to-all-start.2
  36.1 0.6 convert_element_type.62.mix.mix_w
  36.7 0.6 fusion.12
  37.5 0.7 broadcast_in_dim_reshape.6.mix_row
  38.3 0.7 broadcast_in_dim_reshape.7.mix_row
  39.0 1.0 copy.83.id_col
  41.1 15.1 %all-to-all-done.2 = bf16[4,256,768]{2,1,0:T(8,128)(2,1)} async-done(((bf16[4,256,768]{2,1,0:T(8,128)(2,1)}), bf16[4,256,768]{2,1,0:T(8,128)(2,1)}, u32[]{:S(2)}, u32[]{:S(2)}) %all-to-all-start.2) | async-done | bytes 1572896 | tf_op jit(solution)/shard_map/all_to_all | solution.py:233
  56.2 2.6 copy.107
  58.7 2.1 copy.106
  60.8 2.2 multiply_convert_fusion.2
  63.0 1.5 convolution_convert_fusion.1.v
  64.9 2.6 convolution_convert_fusion.2
  67.5 2.6 convolution_convert_fusion.3.q
  70.1 2.6 copy.84.q_t
  72.7 2.6 copy.85.k
  75.3 1.6 copy.86.v_t
  76.9 25.8 %softmaxes.1.soft = bf16[12,1024,1024]{2,1,0:T(8,128)(2,1)} custom-call(f32[12,12]{1,0:T(8,128)} %get-tuple-element.85.mix.mix_l, s32[1,1024]{1,0:T(1,128)} %constant_dynamic-slice_fusion.id_row, s32[1024,1]{1,0:T(8,128)} %copy.83.id_col, bf16[768,1024]{1,0:T(8,128)(2,1)} %copy.84.q_t, bf16[1024,768]{1,0:T(8,128)(2,1)} %copy.85.k), custom_call_target="tpu_custom_call" | custom-call | tf_op jit(solution)/shard_map/softmaxes/pallas_call | solution.py:170
  102.7 20.7 %attend.1 = bf16[1024,768]{1,0:T(8,128)(2,1)} custom-call(f32[12,12]{1,0:T(8,128)} %convert_element_type.62.mix.mix_w, bf16[12,1024,1024]{2,1,0:T(8,128)(2,1)} %softmaxes.1.soft, bf16[768,1024]{1,0:T(8,128)(2,1)} %copy.86.v_t), custom_call_target="tpu_custom_call" | custom-call | tf_op jit(solution)/shard_map/attend/pallas_call | solution.py:179
  123.4 3.9 multiply_reduce_fusion.4
  127.4 8.4 %fusion.14 = f32[1024,3072]{1,0:T(8,128)S(1)} fusion(bf16[768,3072]{1,0:T(8,128)(2,1)} %param.23, f32[1024,768]{0,1:T(8,128)S(1)} %get-tuple-element.87, f32[768]{0:T(1024)S(1)} %copy-done.20, f32[1024]{0:T(1024)S(1)} %add_rsqrt_fusion), kind=kOutput, calls=%fused_computation.41 | convolution fusion | flops 4834197504 | bytes 20454400 | tf_op jit(solution)/shard_map/dot_general | solution.py:26
  135.8 11.7 %fusion.15 = f32[3072,768]{1,0:T(8,128)} fusion(bf16[1024,768]{1,0:T(8,128)(2,1)} %bitcast.5, f32[1024,3072]{1,0:T(8,128)S(1)} %fusion.14), kind=kOutput, calls=%fused_computation.42 | convolution fusion | flops 4860149760 | bytes 23592960 | tf_op jit(solution)/shard_map/dot_general | solution.py:211
  147.6 15.3 %fusion.6 = bf16[1024,3072]{1,0:T(8,128)(2,1)} fusion(f32[1024,3072]{1,0:T(8,128)S(1)} %fusion.14, bf16[1024,768]{1,0:T(8,128)(2,1)} %bitcast.5, bf16[3072,768]{1,0:T(8,128)(2,1)} %param.24), kind=kOutput, calls=%fused_computation.8 | convolution fusion | flops 4894752768 | bytes 25165824 | tf_op jit(solution)/shard_map/dot_general | solution.py:215
  162.9 9.6 %multiply_reduce_fusion = (f32[768]{0:T(1024)S(1)}, f32[1024]{0:T(1024)S(1)}, f32[1024,768]{0,1:T(8,128)S(1)}) fusion(f32[1024,768]{0,1:T(8,128)S(1)} %get-tuple-element.87, f32[1024]{0:T(1024)S(1)} %add_rsqrt_fusion, f32[768]{0:T(1024)S(1)} %copy-done.20, bf16[1024,3072]{1,0:T(8,128)(2,1)} %fusion.6, bf16[768,3072]{1,0:T(8,128)(2,1)} %param.23), kind=kOutput, calls=%fused_computation.10 | convolution fusion | flops 4836554752 | bytes 17315840 | tf_op jit(solution)/shard_map/dot_general | solution.py:215
  172.5 7.6 %fusion.13 = f32[768,3072]{1,0:T(8,128)} fusion(bf16[1024,3072]{1,0:T(8,128)(2,1)S(1)} %copy-done.34, f32[1024,768]{0,1:T(8,128)S(1)} %get-tuple-element.87, f32[768]{0:T(1024)S(1)} %copy-done.20, f32[1024]{0:T(1024)S(1)} %add_rsqrt_fusion), kind=kOutput, calls=%fused_computation.40 | convolution fusion | flops 4834197504 | bytes 18881536 | tf_op jit(solution)/shard_map/dot_general | solution.py:211
  180.1 1.0 subtract_add_fusion
  181.5 2.8 fusion.9
  184.4 1.5 convolution_convert_fusion.g
  185.8 1.6 copy.91.g_t
  187.5 21.2 %value_grads.1 = (bf16[1024,768]{1,0:T(8,128)(2,1)}, f32[12,1,768]{2,1,0:T(1,128)}) custom-call(f32[12,1,768]{2,1,0:T(1,128)} %broadcast_in_dim_reshape.7.mix_row, bf16[12,1024,1024]{2,1,0:T(8,128)(2,1)} %softmaxes.1.soft, bf16[1024,768]{1,0:T(8,128)(2,1)} %copy-done.3, bf16[1024,768]{1,0:T(8,128)(2,1)} %copy-done.7), custom_call_target="tpu_custom_call" | custom-call | tf_op jit(solution)/shard_map/value_grads/pallas_call | solution.py:185
  208.7 50.7 %query_grads.1 = (bf16[1024,768]{1,0:T(8,128)(2,1)}, bf16[12,1024,1024]{2,1,0:T(8,128)(2,1)}, f32[12,768,1]{2,1,0:T(8,128)}) custom-call(f32[12,12]{1,0:T(8,128)} %convert_element_type.62.mix.mix_w, f32[12,12]{1,0:T(8,128)} %get-tuple-element.85.mix.mix_l, bf16[12,1024,1024]{2,1,0:T(8,128)(2,1)} %softmaxes.1.soft, bf16[1024,768]{1,0:T(8,128)(2,1)} %copy-done.3, ...), custom_call_target="tpu_custom_call" | custom-call | tf_op jit(solution)/shard_map/query_grads/pallas_call | solution.py:192
  259.4 20.4 %key_grads.1 = bf16[1024,768]{1,0:T(8,128)(2,1)} custom-call(f32[12,1,768]{2,1,0:T(1,128)} %broadcast_in_dim_reshape.6.mix_row, bf16[12,1024,1024]{2,1,0:T(8,128)(2,1)} %get-tuple-element.18.grad_logits, bf16[1024,768]{1,0:T(8,128)(2,1)} %convolution_convert_fusion.3.q), custom_call_target="tpu_custom_call" | custom-call | tf_op jit(solution)/shard_map/key_grads/pallas_call | solution.py:202
  279.9 4.3 fusion.19
  284.2 2.8 fusion.20
  287.0 2.8 fusion.18
  289.8 10.8 %fusion.8 = bf16[1,1024,768]{1,2,0:T(8,128)(2,1)S(1)} fusion(f32[1024,768]{0,1:T(8,128)} %copy-done.2, bf16[3072,768]{1,0:T(8,128)(2,1)} %param.24, f32[1024,3072]{1,0:T(8,128)} %copy-done.4), kind=kOutput, calls=%fused_computation.28 | convolution fusion | flops 4861722624 | bytes 22020096 | tf_op jit(solution)/shard_map/dot_general | solution.py:26
  300.6 6.1 copy.88
  307.2 11.3 %reduce.6 = bf16[1024,768]{1,0:T(8,128)(2,1)S(1)} reduce(bf16[1024,1,768]{2,1,0:T(2,128)(2,1)} %bitcast.58, bf16[]{:T(256)} %broadcast.105), dimensions={1}, to_apply=%bitcast.21.reduce_sub_computation | reduce | bytes 3145730
  318.5 1.8 reshape.108
  320.4 4.5 all-to-all-start.1
  324.9 2.9 fusion.17
  327.8 1.4 fusion.16
  330.2 2.0 multiply_reduce_fusion.1
  332.2 0.9 fusion.7
  333.1 5.9 copy.97
  339.0 11.4 %reduce.7 = bf16[1024,768]{1,0:T(8,128)(2,1)S(1)} reduce(bf16[1024,1,768]{2,1,0:T(2,128)(2,1)} %bitcast.59, bf16[]{:T(256)} %broadcast.105), dimensions={1}, to_apply=%bitcast.23.reduce_sub_computation | reduce | bytes 3145730
  350.5 1.9 reshape.110
  352.4 3.6 all-to-all-start.3
  356.0 3.7 reduce.4
  360.1 58.6 %all-reduce = (f32[768]{0:T(1024)}, f32[12,12]{0,1:T(8,128)S(1)}, f32[12,12]{1,0:T(8,128)}, f32[768]{0:T(1024)}) all-reduce(f32[768]{0:T(1024)S(1)} %get-tuple-element.72, f32[12,12]{0,1:T(8,128)S(1)} %multiply_bitcast_fusion, f32[12,12]{1,0:T(8,128)S(1)} %reduce_sum.78, ...), channel_id=1, replica_groups=mesh['rows'=8,'seq'=4] {'rows','seq'}, use_global_device_ids=true, to_apply=%region_5.0 | all-reduce | flops 1824 | bytes 14592 | tf_op jit(solution)/shard_map/psum | solution.py:300
  418.7 0.7 copy.99
  419.4 4.5 reshape.109
  423.8 3.4 copy.108
  427.2 2.8 reshape.111
  430.0 3.3 copy.109
  433.3 294.6 %all-reduce.4.cloned.1.call-done = (f32[768,768]{1,0:T(8,128)}, f32[768,768]{1,0:T(8,128)}, f32[768,768]{1,0:T(8,128)}, f32[768,768]{1,0:T(8,128)}, f32[768,3072]{1,0:T(8,128)}, /*index=5*/f32[3072,768]{1,0:T(8,128)}) async-done(((f32[768,768]{1,0:T(8,128)}, f32[768,768]{1,0:T(8,128)}, f32[768,768]{1,0:T(8,128)}, f32[768,768]{1,0:T(8,128)}, f32[768,3072]{1,0:T(8,128)}, /*index=5*/f32[3072,768]{1,0:T(8,128)}), ...) | async-done | bytes 28311568 | tf_op jit(solution)/shard_map/psum | solution.py:300
  727.9 3.4 copy.117
  731.3 1.4 copy.118
  732.7 1.1 copy-done.13
  733.8 1.4 copy.119
  735.2 1.1 copy-done.12
  736.3 1.4 copy.120
  737.8 9.3 %copy.121 = f32[768,3072]{1,0:T(8,128)} copy(f32[768,3072]{1,0:T(8,128)} %get-tuple-element.100) | data formatting | bytes 18874368
  747.1 3.7 copy.122
  (97 shorter events, 4.2 us)
Async XLA Ops:
  7.2 55.8 %copy-start = (bf16[768,768]{1,0:T(8,128)(2,1)S(1)}, bf16[768,768]{1,0:T(8,128)(2,1)}, u32[]{:S(2)}) copy-start(bf16[768,768]{1,0:T(8,128)(2,1)} %param.18) | copy-start | bytes 3538948
  7.2 28.9 %copy-start.26 = (bf16[12,12]{1,0:T(8,128)(2,1)S(1)}, bf16[12,12]{1,0:T(8,128)(2,1)}, u32[]{:S(2)}) copy-start(bf16[12,12]{1,0:T(8,128)(2,1)} %param.21) | copy-start | bytes 868
  7.2 29.5 %copy-start.27 = (bf16[12,12]{1,0:T(8,128)(2,1)S(1)}, bf16[12,12]{1,0:T(8,128)(2,1)}, u32[]{:S(2)}) copy-start(bf16[12,12]{1,0:T(8,128)(2,1)} %param.20) | copy-start | bytes 868
  7.2 31.8 %copy-start.28 = (s32[4,1024]{1,0:T(4,128)S(1)}, s32[4,1024]{1,0:T(4,128)}, u32[]{:S(2)}) copy-start(s32[4,1024]{1,0:T(4,128)} %param.14) | copy-start | bytes 49156
  31.7 24.5 %all-to-all-start.2 = ((bf16[4,256,768]{2,1,0:T(8,128)(2,1)}), bf16[4,256,768]{2,1,0:T(8,128)(2,1)}, u32[]{:S(2)}, u32[]{:S(2)}) async-start(bf16[4,256,768]{2,1,0:T(8,128)(2,1)} %param.25), calls=%async_computation.2 | async-start | bytes 3145728 | tf_op jit(solution)/shard_map/all_to_all | solution.py:233
  36.0 691.9 %all-reduce.4.cloned.1.call-start = ((), (), s32[]{:S(2)}) async-start(), calls=%async_computation.4 | async-start | bytes 56623104 | tf_op jit(solution)/shard_map/psum | solution.py:300
  41.0 19.8 %copy-start.21 = (f32[1,2,4,128]{3,1,2,0:T(2,128)}, f32[1,2,4,128]{3,1,2,0:T(2,128)S(1)}, u32[]{:S(2)}) copy-start(f32[1,2,4,128]{3,1,2,0:T(2,128)S(1)} %copy.110) | copy-start | bytes 12292
  58.7 2.1 copy-start.23
  63.0 4.5 copy-start.16
  63.0 1.8 copy-start.31
  64.9 10.4 %copy-start.3 = (bf16[1024,768]{1,0:T(8,128)(2,1)}, bf16[1024,768]{1,0:T(8,128)(2,1)S(1)}, u32[]{:S(2)}) copy-start(bf16[1024,768]{1,0:T(8,128)(2,1)S(1)} %convolution_convert_fusion.1.v) | copy-start | bytes 4718596
  64.9 2.6 copy-start.32
  102.7 20.7 %copy-start.18 = (bf16[768,768]{1,0:T(8,128)(2,1)S(1)}, bf16[768,768]{1,0:T(8,128)(2,1)}, u32[]{:S(2)}) copy-start(bf16[768,768]{1,0:T(8,128)(2,1)} %param.19) | copy-start | bytes 3538948
  123.4 4.0 copy-start.20
  127.4 52.7 %copy-start.2 = (f32[1024,768]{0,1:T(8,128)}, f32[1024,768]{0,1:T(8,128)S(1)}, u32[]{:S(2)}) copy-start(f32[1024,768]{0,1:T(8,128)S(1)} %get-tuple-element.87) | copy-start | bytes 9437188
  135.8 11.7 %copy-start.4 = (f32[1024,3072]{1,0:T(8,128)}, f32[1024,3072]{1,0:T(8,128)S(1)}, u32[]{:S(2)}) copy-start(f32[1024,3072]{1,0:T(8,128)S(1)} %fusion.14) | copy-start | bytes 37748740
  162.9 9.6 %copy-start.34 = (bf16[1024,3072]{1,0:T(8,128)(2,1)S(1)}, bf16[1024,3072]{1,0:T(8,128)(2,1)}, u32[]{:S(2)}) copy-start(bf16[1024,3072]{1,0:T(8,128)(2,1)} %fusion.6) | copy-start | bytes 18874372
  172.5 7.6 %copy-start.8 = (bf16[1024,768]{0,1:T(8,128)(2,1)S(1)}, bf16[1024,768]{0,1:T(8,128)(2,1)}, u32[]{:S(2)}) copy-start(bf16[1024,768]{0,1:T(8,128)(2,1)} %copy.107) | copy-start | bytes 4718596
  180.1 1.4 copy-start.9
  181.5 2.9 copy-start.5
  181.5 2.9 copy-start.19
  185.8 1.7 copy-start.7
  259.4 20.4 %copy-start.17 = (bf16[1024,768]{0,1:T(8,128)(2,1)S(1)}, bf16[1024,768]{0,1:T(8,128)(2,1)}, u32[]{:S(2)}) copy-start(bf16[1024,768]{0,1:T(8,128)(2,1)} %copy-done.16) | copy-start | bytes 4718596
  279.8 4.3 copy-start.10
  284.2 2.8 copy-start.29
  320.4 4.5 copy-start.15
  320.4 32.0 %all-to-all-start.1 = ((bf16[4,2,98304]{2,1,0:T(2,128)(2,1)}), bf16[4,2,98304]{2,1,0:T(2,128)(2,1)}, u32[]{:S(2)}, u32[]{:S(2)}) async-start(bf16[4,2,98304]{2,1,0:T(2,128)(2,1)} %reshape.108), calls=%async_computation.1 | async-start | bytes 3145728 | tf_op jit(solution)/shard_map/all_to_all | solution.py:237
  324.9 2.9 copy-start.30
  324.9 2.9 copy-start.33
  327.8 1.9 copy-start.1
  327.8 2.4 copy-start.11
  327.8 2.4 copy-start.22
  327.8 2.4 copy-start.24
  330.2 2.0 copy-start.6
  350.5 5.5 copy-start.25
  352.4 74.9 %all-to-all-start.3 = ((bf16[4,2,98304]{2,1,0:T(2,128)(2,1)}), bf16[4,2,98304]{2,1,0:T(2,128)(2,1)S(1)}, u32[]{:S(2)}, u32[]{:S(2)}) async-start(bf16[4,2,98304]{2,1,0:T(2,128)(2,1)} %reshape.110), calls=%async_computation.3 | async-start | bytes 3145728 | tf_op jit(solution)/shard_map/all_to_all | solution.py:237
  727.9 3.4 copy-start.14
  731.3 2.5 copy-start.13
  733.8 2.5 copy-start.12
  736.3 10.7 %slice-start = ((s8[9437184]{0:T(1024)(128)(4,1)}), s8[4194304]{0:T(1024)(128)(4,1)S(1)}, s32[]{:S(2)}) async-start(s8[9437184]{0:T(1024)(128)(4,1)} %bitcast.62), calls=%async_computation.5 | async-start | bytes 8388608
  737.7 9.3 %slice-start.1 = ((s8[9437184]{0:T(1024)(128)(4,1)}), s8[4194304]{0:T(1024)(128)(4,1)S(1)}, s32[]{:S(2)}) async-start(s8[9437184]{0:T(1024)(128)(4,1)} %bitcast.62), calls=%async_computation.6 | async-start | bytes 8388608
  737.8 9.3 %slice-start.2 = ((s8[9437184]{0:T(1024)(128)(4,1)}), s8[1048576]{0:T(1024)(128)(4,1)S(1)}, s32[]{:S(2)}) async-start(s8[9437184]{0:T(1024)(128)(4,1)} %bitcast.62), calls=%async_computation.7 | async-start | bytes 2097152
Sparse Core Ops, SparseCore 0:
  289.9 437.9 all-reduce.3
